TPU v7x, 32 devices: a whole 2x2x4 slice. The times are simulated.
32 devices in a mesh: dp: 8 (over z, y), tensor: 4 (over x, core).
Axes of the slice: x: 2, y: 2, z: 4, core: 2. Of those that a mesh axis runs over, the one named last changes fastest.
Arguments:
- prompt_hidden: bfloat16 [1024, 5120], P('dp'), may hold values from -6 to 6
- w_key: bfloat16 [5120, 1024], P(None, 'tensor'), may hold values from -0.078125 to 0.078125
- w_value: bfloat16 [5120, 1024], P(None, 'tensor'), may hold values from -0.078125 to 0.078125
- resp_query: bfloat16 [1024, 8192], P('dp', 'tensor'), may hold values from -160 to 160
- resp_kv: bfloat16 [2, 1024, 1024], P(None, 'dp', 'tensor'), may hold values from -6 to 6
- cotangent: bfloat16 [1024, 8192], P('dp', 'tensor'), may hold values from -6 to 6
- prompt_len: int32 [8], replicated, may hold values from 32 to 128, as said below
- resp_len: int32 [8], P('dp'), may hold values from 16 to 128, as said below
- offsets: int32 [8], P('dp'), may hold values from 0 to 3, as said below
- advantage: int32 [8], P('dp'), may hold values from -2 to 2
Outputs:
- attn_out: bfloat16 [1024, 8192], P('dp', 'tensor')
- grad_query: bfloat16 [1024, 8192], P('dp', 'tensor')
- grad_resp_kv: bfloat16 [2, 1024, 1024], P(None, 'dp', 'tensor')
- grad_prompt_hidden: bfloat16 [1024, 5120], P('dp', 'tensor')
Inputs may be any that keep to these rules, and one draw needn't show every extreme that they name: `prompt_len`: some prompt has exactly 128 tokens. `resp_len`: some slot's response has exactly 128 tokens. `offsets`: some slot has offset 0 and some slot offset 4 - 1.
All inputs are finite; a program needn't handle non-finite values.
Results may differ from a plain program's by a relative error of at most 0.012.
Values may be sent and summed in bfloat16 or wider, within the bound.
A program may use at most 64 MiB of HBM per device.

v0:
```python
import jax
import jax.numpy as jnp
from jax import lax
from jax.sharding import PartitionSpec as P

HD = 128


MASKED_SCORE = -1e30


def passed_along(value, axis, steps):
    count = lax.axis_size(axis)
    pairs = [(source, (source + steps) % count) for source in range(count)]
    return lax.ppermute(value, axis, pairs)


def fan_out(prompt_kv):
    window = min(8, lax.axis_size("dp") // 2)
    blocks = [prompt_kv]
    for distance in range(1, window):
        blocks.append(passed_along(prompt_kv, "dp", distance))
    return jnp.stack(blocks)


def fan_in(per_offset):
    window = per_offset.shape[0]
    summed = per_offset[0]
    for distance in range(1, window):
        summed = summed + passed_along(
            per_offset[distance].astype(jnp.bfloat16), "dp", -distance
        ).astype(jnp.float32)
    return summed


def local(
    prompt_hidden,
    w_key,
    w_value,
    resp_query,
    resp_kv,
    cotangent,
    prompt_len,
    resp_len,
    offsets,
    advantage,
):
    slots_dev = resp_len.shape[0]
    slot_rows = resp_query.shape[0] // slots_dev
    kv_width = w_key.shape[1]
    kv_heads = kv_width // HD
    group_size = resp_query.shape[1] // HD // kv_heads
    prefix_rows = prompt_hidden.shape[0]
    score_scale = HD ** (-0.5)
    contract = (((1,), (1,)), ((), ()))
    prompt_keys = jnp.dot(prompt_hidden, w_key, preferred_element_type=jnp.float32).astype(
        jnp.bfloat16
    )
    prompt_values = jnp.dot(prompt_hidden, w_value, preferred_element_type=jnp.float32).astype(
        jnp.bfloat16
    )
    prompt_kv = jnp.stack([prompt_keys, prompt_values])
    queries = resp_query.reshape(slots_dev, slot_rows, kv_heads, group_size, HD)
    own_keys = resp_kv[0].reshape(slots_dev, slot_rows, kv_heads, HD)
    own_values = resp_kv[1].reshape(slots_dev, slot_rows, kv_heads, HD)
    position = jnp.arange(slot_rows)
    row_valid = position[None, :] < resp_len[:, None]
    causal = (position[:, None] >= position[None, :])[None, :, None, None, :]
    owner_rank = (lax.axis_index("dp") - offsets) % lax.axis_size("dp")
    owner_match = jnp.arange(prompt_len.shape[0])[None, :] == owner_rank[:, None]
    chosen_len = jnp.sum(jnp.where(owner_match, prompt_len[None, :], 0), axis=1)
    blocks = fan_out(prompt_kv)
    selector = offsets[:, None] == jnp.arange(blocks.shape[0])[None, :]
    chosen = jnp.einsum(
        "sw,wcpe->scpe", selector.astype(jnp.bfloat16), blocks, preferred_element_type=jnp.float32
    ).astype(jnp.bfloat16)
    pre_keys = chosen[:, 0].reshape(slots_dev, prefix_rows, kv_heads, HD)
    pre_values = chosen[:, 1].reshape(slots_dev, prefix_rows, kv_heads, HD)
    scores = (
        jnp.einsum("srkgd,spkd->srkgp", queries, pre_keys, preferred_element_type=jnp.float32)
        * score_scale
    )
    prefix_ok = (jnp.arange(prefix_rows)[None, :] < chosen_len[:, None])[:, None, None, None, :]
    selector, pre_keys, pre_values, pre_scores = (
        selector,
        pre_keys,
        pre_values,
        jnp.where(prefix_ok, scores, MASKED_SCORE),
    )
    scores = (
        jnp.einsum("srkgd,sukd->srkgu", queries, own_keys, preferred_element_type=jnp.float32)
        * score_scale
    )
    own_scores = jnp.where(causal, scores, MASKED_SCORE)
    top = jnp.maximum(pre_scores.max(-1), own_scores.max(-1))
    log_total = top + jnp.log(
        jnp.sum(jnp.exp(pre_scores - top[..., None]), -1)
        + jnp.sum(jnp.exp(own_scores - top[..., None]), -1)
    )
    pre_probs = jnp.exp(pre_scores - log_total[..., None])
    own_probs = jnp.exp(own_scores - log_total[..., None])
    pre_weights = pre_probs.astype(jnp.bfloat16)
    own_weights = own_probs.astype(jnp.bfloat16)
    valid_mask = row_valid[:, :, None, None, None].astype(jnp.float32)
    output = jnp.einsum(
        "srkgp,spkd->srkgd", pre_weights, pre_values, preferred_element_type=jnp.float32
    )
    output = (
        output
        + jnp.einsum(
            "srkgu,sukd->srkgd", own_weights, own_values, preferred_element_type=jnp.float32
        )
    ) * valid_mask
    attn_out = output.astype(jnp.bfloat16).reshape(slots_dev * slot_rows, -1)
    row_factor = (advantage[:, None] * row_valid.astype(jnp.int32)).astype(jnp.bfloat16)
    grad_out = cotangent.reshape(queries.shape) * row_factor[:, :, None, None, None]
    grad_pre = jnp.einsum(
        "srkgd,spkd->srkgp", grad_out, pre_values, preferred_element_type=jnp.float32
    )
    grad_own = jnp.einsum(
        "srkgd,sukd->srkgu", grad_out, own_values, preferred_element_type=jnp.float32
    )
    row_delta = jnp.sum(grad_out.astype(jnp.float32) * output, -1)
    pre_dscores = (pre_probs * (grad_pre - row_delta[..., None])).astype(jnp.bfloat16)
    own_dscores = (own_probs * (grad_own - row_delta[..., None])).astype(jnp.bfloat16)
    grad_queries = jnp.einsum(
        "srkgp,spkd->srkgd", pre_dscores, pre_keys, preferred_element_type=jnp.float32
    )
    grad_queries = (
        grad_queries
        + jnp.einsum("srkgu,sukd->srkgd", own_dscores, own_keys, preferred_element_type=jnp.float32)
    ) * score_scale
    grad_key_own = (
        jnp.einsum("srkgu,srkgd->sukd", own_dscores, queries, preferred_element_type=jnp.float32)
        * score_scale
    )
    grad_value_own = jnp.einsum(
        "srkgu,srkgd->sukd", own_weights, grad_out, preferred_element_type=jnp.float32
    )
    grad_resp_kv = jnp.stack(
        [
            grad_key_own.reshape(slots_dev * slot_rows, kv_width),
            grad_value_own.reshape(slots_dev * slot_rows, kv_width),
        ]
    ).astype(jnp.bfloat16)
    grad_key_pre = (
        jnp.einsum("srkgp,srkgd->spkd", pre_dscores, queries, preferred_element_type=jnp.float32)
        * score_scale
    )
    grad_value_pre = jnp.einsum(
        "srkgp,srkgd->spkd", pre_weights, grad_out, preferred_element_type=jnp.float32
    )
    slot_grads = jnp.stack([grad_key_pre, grad_value_pre], 1).reshape(
        slots_dev, 2, prefix_rows, kv_width
    )
    per_offset = jnp.einsum(
        "sw,scpe->wcpe", selector.astype(jnp.float32), slot_grads, precision=lax.Precision.HIGHEST
    )
    returned = fan_in(per_offset)
    key_grad = returned[0].astype(jnp.bfloat16)
    value_grad = returned[1].astype(jnp.bfloat16)
    partial_grad = lax.dot_general(key_grad, w_key, contract, preferred_element_type=jnp.float32)
    partial_grad = partial_grad + lax.dot_general(
        value_grad, w_value, contract, preferred_element_type=jnp.float32
    )
    grad_prompt = lax.psum_scatter(
        partial_grad.astype(jnp.bfloat16), "tensor", scatter_dimension=1, tiled=True
    )
    return (
        attn_out,
        grad_queries.astype(jnp.bfloat16).reshape(slots_dev * slot_rows, -1),
        grad_resp_kv,
        grad_prompt,
    )


def solution(mesh):
    placed = (
        P("dp", None),
        P(None, "tensor"),
        P(None, "tensor"),
        P("dp", "tensor"),
        P(None, "dp", "tensor"),
        P("dp", "tensor"),
        P(),
        P("dp"),
        P("dp"),
        P("dp"),
    )
    return jax.shard_map(
        local,
        mesh=mesh,
        in_specs=placed,
        out_specs=(
            P("dp", "tensor"),
            P("dp", "tensor"),
            P(None, "dp", "tensor"),
            P("dp", "tensor"),
        ),
        check_vma=False,
    )
```

profile of v0, /device:TPU:0, one launch (start us, length us, event | category | flops | bytes accessed | tf_op | source)
XLA Modules:
  0.0 92.7 jit_solution(14276976099941309354)
XLA Ops:
  7.2 2.8 %fusion.26 = bf16[1,128,256]{2,1,0:T(8,128)(2,1)S(1)} fusion(bf16[128,5120]{1,0:T(8,128)(2,1)} %param.10, bf16[5120,256]{1,0:T(8,128)(2,1)} %param.12), kind=kOutput, calls=%fused_computation.38 | convolution fusion | flops 335577088 | bytes 3997696 | tf_op jit(solution)/shard_map/dot_general | solution.py:59
  10.1 0.4 copy-done.5
  10.5 0.5 fusion.25
  11.0 0.7 fusion.60
  11.7 3.0 %collective-permute-start.1 = (bf16[2,128,256]{2,1,0:T(8,128)(2,1)}, bf16[2,128,256]{2,1,0:T(8,128)(2,1)}, u32[]{:S(2)}, u32[]{:S(2)}) collective-permute-start(bf16[2,128,256]{2,1,0:T(8,128)(2,1)} %get-tuple-element.26), channel_id=1, source_target_pairs={{0,8},{4,12},{8,16},{12,20},{16,24},{20,28},{24,0},{28,4},{1,9},{5... | collective-permute-start | bytes 393224 | tf_op jit(solution)/shard_map/ppermute | solution.py:15
  14.7 1.5 %collective-permute-start = (bf16[2,128,256]{2,1,0:T(8,128)(2,1)}, bf16[2,128,256]{2,1,0:T(8,128)(2,1)}, u32[]{:S(2)}, u32[]{:S(2)}) collective-permute-start(bf16[2,128,256]{2,1,0:T(8,128)(2,1)} %get-tuple-element.26), channel_id=1, source_target_pairs={{0,4},{4,8},{8,12},{12,16},{16,20},{20,24},{24,28},{28,0},{1,5},{5... | collective-permute-start | bytes 393224 | tf_op jit(solution)/shard_map/ppermute | solution.py:15
  16.2 2.5 %collective-permute-start.2 = (bf16[2,128,256]{2,1,0:T(8,128)(2,1)}, bf16[2,128,256]{2,1,0:T(8,128)(2,1)}, u32[]{:S(2)}, u32[]{:S(2)}) collective-permute-start(bf16[2,128,256]{2,1,0:T(8,128)(2,1)} %get-tuple-element.26), channel_id=1, source_target_pairs={{0,12},{4,16},{8,20},{12,24},{16,28},{20,0},{24,4},{28,8},{1,13},{... | collective-permute-start | bytes 393224 | tf_op jit(solution)/shard_map/ppermute | solution.py:15
  20.1 0.6 fusion.58
  20.7 0.6 iota_compare_fusion.1
  21.4 0.5 compare_convert_fusion
  21.9 0.1 copy.104
  22.0 1.3 %copy.105 = bf16[128,2048]{0,1:T(8,128)(2,1)S(1)} copy(bf16[128,2048]{1,0:T(8,128)(2,1)} %param.13) | data formatting | bytes 1048576 | tf_op jit(solution)/shard_map/reshape.12
  23.4 1.3 %fusion.64 = (f32[128,2,8]{0,2,1:T(8,128)S(1)}, f32[1,128,2,8,128]{1,4,3,2,0:T(8,128)}) fusion(bf16[128,2,128,1]{0,2,3,1:T(8,128)(2,1)S(1)} %bitcast.249, bf16[128,2,8,128]{0,3,2,1:T(8,128)(2,1)S(1)} %bitcast.243, pred[128,128]{0,1:T(8,128)(4,1)S(1)} %iota_compare_fusion), kind=kOutput, calls=%fused_computation.96 | convolution fusion | flops 67893248 | bytes 1662976 | tf_op jit(solution)/shard_map/srkgd,sukd->srkgu/dot_general | solution.py:91
  24.7 0.6 compare_convert_fusion.1
  25.9 0.1 copy.47
  26.0 1.3 %copy.101 = bf16[128,2048]{0,1:T(8,128)(2,1)S(1)} copy(bf16[128,2048]{1,0:T(8,128)(2,1)} %param.15) | data formatting | bytes 1048576 | tf_op jit(solution)/shard_map/reshape | solution.py:116
  27.4 2.5 %collective-permute-done.2 = bf16[2,128,256]{2,1,0:T(8,128)(2,1)} collective-permute-done((bf16[2,128,256]{2,1,0:T(8,128)(2,1)}, bf16[2,128,256]{2,1,0:T(8,128)(2,1)}, u32[]{:S(2)}, u32[]{:S(2)}) %collective-permute-start.2) | collective-permute-done | bytes 131104 | tf_op jit(solution)/shard_map/ppermute | solution.py:15
  29.9 1.1 %pad_maximum_fusion = bf16[4,2,128,256]{3,2,1,0:T(8,128)(2,1)S(1)} fusion(bf16[1,2,128,256]{3,2,1,0:T(8,128)(2,1)} %bitcast.8, bf16[1,2,128,256]{3,2,1,0:T(8,128)(2,1)} %bitcast.7, bf16[1,2,128,256]{3,2,1,0:T(8,128)(2,1)} %bitcast.6, bf16[1,2,128,256]{3,2,1,0:T(8,128)(2,1)S(1)} %get-tuple-element.25), kind=kLoop, calls=%fused_computation.48 | loop fusion | flops 786432 | bytes 1048576 | tf_op jit(solution)/shard_map/stack | solution.py:23
  31.0 1.2 %fusion.31 = bf16[1,2,128,256]{3,0,2,1:T(2,128)(2,1)} fusion(bf16[4,2,128,256]{3,2,1,0:T(8,128)(2,1)S(1)} %pad_maximum_fusion, s32[]{:T(128)} %bitcast.235), kind=kOutput, calls=%fused_computation.50 | convolution fusion | flops 524292 | bytes 655364 | tf_op jit(solution)/shard_map/sw,wcpe->scpe/dot_general | solution.py:74
  32.2 1.1 %copy.71 = bf16[1,2,128,256]{2,3,1,0:T(8,128)(2,1)S(1)} copy(bf16[1,2,128,256]{3,0,2,1:T(2,128)(2,1)} %fusion.31) | data formatting | bytes 262144 | tf_op jit(solution)/shard_map/sw,wcpe->scpe/dot_general | solution.py:74
  33.4 0.6 copy-done.8
  34.0 1.4 %fusion.63 = (f32[128,2,8]{0,2,1:T(8,128)S(1)}, f32[1,128,2,8,128]{1,4,3,2,0:T(8,128)S(1)}) fusion(bf16[128,2,128,1]{0,2,3,1:T(8,128)(2,1)S(1)} %bitcast.253, bf16[128,2,8,128]{0,3,2,1:T(8,128)(2,1)} %bitcast.244, pred[128]{0:T(512)(128)(4,1)S(1)} %iota_compare_fusion.1), kind=kOutput, calls=%fused_computation.95 | convolution fusion | flops 67893248 | bytes 1646720 | tf_op jit(solution)/shard_map/srkgd,spkd->srkgp/dot_general | solution.py:80
  35.4 0.4 exponential_reduce_fusion
  35.8 0.3 fusion.48
  36.2 0.3 fusion.33
  36.5 1.9 %multiply_reduce_fusion = (f32[128,2,8]{0,2,1:T(8,128)S(1)}, bf16[1,128,2,8,128]{1,4,3,2,0:T(8,128)(2,1)}) fusion(bf16[1,128,2,8,128]{1,4,3,2,0:T(8,128)(2,1)S(1)} %bitcast.239, bf16[128]{0:T(256)(128)(2,1)} %copy-done.11, f32[128]{0:T(128)S(1)} %copy-done.14, f32[2,128,128,8]{2,1,3,0:T(8,128)S(1)} %fusion.48, bf16[128,2,128,1]{0,2,3,1:T(8,128)(2,1)S(1)} %bitcast.251, ...), kind=kOutput, calls=%fused_computation.39 | convolution fusion | flops 69466112 | bytes 3228416 | tf_op jit(solution)/shard_map/srkgu,sukd->srkgd/dot_general | solution.py:110
  38.4 0.4 fusion.19
  38.8 0.3 fusion.22
  39.1 0.5 copy-done.6
  39.7 0.8 copy.66
  40.5 1.2 %fusion.46 = (bf16[4,2,128,256]{3,2,1,0:T(8,128)(2,1)S(1)}, f32[4,2,128,256]{3,2,1,0:T(8,128)S(1)}) fusion(f32[2,128,256]{2,1,0:T(8,128)} %copy.66, f32[4]{0:T(128)} %compare_convert_fusion.1), kind=kLoop, calls=%fused_computation.68 | loop fusion | flops 524288 | bytes 1835024 | tf_op jit(solution)/shard_map/convert.5
  41.8 0.5 collective-permute-start.5
  42.3 1.2 %collective-permute-start.4 = (bf16[2,128,256]{2,1,0:T(8,128)(2,1)S(1)}, bf16[2,128,256]{2,1,0:T(8,128)(2,1)S(1)}, u32[]{:S(2)}, u32[]{:S(2)}) collective-permute-start(bf16[2,128,256]{2,1,0:T(8,128)(2,1)S(1)} %get-tuple-element.18), channel_id=1, source_target_pairs={{0,24},{4,28},{8,0},{12,4},{16,8},{20,12},{24,16},{28,20},{1,25},{... | collective-permute-start | bytes 393224 | tf_op jit(solution)/shard_map/ppermute | solution.py:15
  43.5 6.5 %collective-permute-done.3 = bf16[2,128,256]{2,1,0:T(8,128)(2,1)S(1)} collective-permute-done((bf16[2,128,256]{2,1,0:T(8,128)(2,1)S(1)}, bf16[2,128,256]{2,1,0:T(8,128)(2,1)S(1)}, u32[]{:S(2)}, u32[]{:S(2)}) %collective-permute-start.3) | collective-permute-done | bytes 131104 | tf_op jit(solution)/shard_map/ppermute | solution.py:15
  50.0 0.7 collective-permute-done.4
  50.7 1.0 %fusion.53 = f32[128,5120]{1,0:T(8,128)S(1)} fusion(bf16[5120,256]{1,0:T(8,128)(2,1)S(1)} %copy-done, bf16[2,128,256]{2,1,0:T(8,128)(2,1)S(1)} %fusion.41), kind=kOutput, calls=%fused_computation.78 | convolution fusion | flops 335544320 | bytes 5308416 | tf_op jit(solution)/shard_map/dot_general | solution.py:162
  51.7 0.7 copy-done.4
  52.5 2.1 %fusion = bf16[128,5120]{1,0:T(8,128)(2,1)} fusion(f32[128,5120]{1,0:T(8,128)S(1)} %fusion.53, bf16[5120,256]{1,0:T(8,128)(2,1)S(1)} %copy-done.4, bf16[2,128,256]{2,1,0:T(8,128)(2,1)S(1)} %fusion.41), kind=kOutput, calls=%fused_computation.1 | convolution fusion | flops 336855040 | bytes 6619136 | tf_op jit(solution)/shard_map/dot_general | solution.py:163
  54.6 1.5 %fusion.24 = bf16[2,128,128]{2,1,0:T(8,128)(2,1)S(1)} fusion(bf16[128,2,8,128]{0,3,2,1:T(8,128)(2,1)S(1)} %bitcast.241, bf16[128]{0:T(256)(128)(2,1)S(1)} %copy-done.13, f32[1,128,2,8,128]{1,4,3,2,0:T(8,128)} %get-tuple-element.30, f32[128,2,8]{0,2,1:T(8,128)S(1)} %log_add_fusion), kind=kOutput, calls=%fused_computation.34 | convolution fusion | flops 67928064 | bytes 1646848 | tf_op jit(solution)/shard_map/srkgu,srkgd->sukd/dot_general | solution.py:137
  56.2 2.0 %copy.67 = bf16[128,2048]{1,0:T(8,128)(2,1)} copy(bf16[128,2048]{0,1:T(8,128)(2,1)} %bitcast.247) | data formatting | bytes 1048576
  58.3 1.6 %fusion.20 = bf16[128,2,8,128]{0,3,2,1:T(8,128)(2,1)S(1)} fusion(bf16[128,2,128,1]{0,2,3,1:T(8,128)(2,1)S(1)} %bitcast.252, f32[1,128,2,8,128]{1,4,3,2,0:T(8,128)} %get-tuple-element.30, f32[128,2,8]{0,2,1:T(8,128)S(1)} %get-tuple-element.14, f32[128,2,8]{0,2,1:T(8,128)S(1)} %log_add_fusion, bf16[128,2,8,128]{0,3,2,1:T(8,128)(2,1)S(1)} %bitcast.242, ...), kind=kOutput, calls=%fused_computation.27 | convolution fusion | flops 68419584 | bytes 2179328 | tf_op jit(solution)/shard_map/srkgd,sukd->srkgu/dot_general | solution.py:120
  59.9 0.8 copy-done.7
  60.7 1.3 %fusion.23 = bf16[2,128,128]{1,2,0:T(8,128)(2,1)S(1)} fusion(bf16[128,2,8,128]{0,3,2,1:T(8,128)(2,1)S(1)} %fusion.20, bf16[128,2,8,128]{0,3,2,1:T(8,128)(2,1)} %bitcast.245), kind=kOutput, calls=%fused_computation.33 | convolution fusion | flops 67174400 | bytes 1114112 | tf_op jit(solution)/shard_map/srkgu,srkgd->sukd/dot_general | solution.py:134
  62.1 1.3 %fusion.65 = f32[2,128,128,8]{2,1,3,0:T(8,128)S(1)} fusion(bf16[128,2,128,1]{0,2,3,1:T(8,128)(2,1)S(1)} %bitcast.254, bf16[128,2,8,128]{0,3,2,1:T(8,128)(2,1)} %copy-done.6), kind=kOutput, calls=%fused_computation.97 | convolution fusion | flops 67108864 | bytes 1638400 | tf_op jit(solution)/shard_map/srkgp,spkd->srkgd/dot_general | solution.py:126
  63.5 1.3 %fusion.15 = bf16[2,128,128,8]{2,1,3,0:T(8,128)(2,1)S(1)} fusion(f32[2,128,128,8]{2,1,3,0:T(8,128)S(1)} %fusion.65, bf16[128,2,128,1]{0,2,3,1:T(8,128)(2,1)S(1)} %bitcast.250, bf16[128,2,8,128]{0,3,2,1:T(8,128)(2,1)} %copy-done.7), kind=kOutput, calls=%fused_computation.22 | convolution fusion | flops 67895296 | bytes 2162688 | tf_op jit(solution)/shard_map/srkgu,sukd->srkgd/dot_general | solution.py:131
  64.8 1.0 %copy.68 = bf16[128,2048]{1,0:T(8,128)(2,1)} copy(bf16[128,2048]{0,1:T(8,128)(2,1)S(1)} %bitcast.248) | data formatting | bytes 1048576
  65.8 0.7 pad_maximum_fusion.3
  66.5 19.4 %reduce-scatter.2.cloned.1.call-done = bf16[128,1280]{1,0:T(8,128)(2,1)} async-done(((bf16[128,5120]{1,0:T(8,128)(2,1)}), bf16[128,1280]{1,0:T(8,128)(2,1)}) %reduce-scatter.2.cloned.1.call-update) | async-done | bytes 327696 | tf_op jit(solution)/shard_map/reduce_scatter | solution.py:166
  (45 shorter events, 0.6 us)
Async XLA Ops:
  7.2 2.9 %copy-start = (bf16[5120,256]{1,0:T(8,128)(2,1)S(1)}, bf16[5120,256]{1,0:T(8,128)(2,1)}, u32[]{:S(2)}) copy-start(bf16[5120,256]{1,0:T(8,128)(2,1)} %param.11) | copy-start | bytes 7864324
  7.2 78.7 %reduce-scatter.2.cloned.1.call-start = ((), (), s32[]{:S(2)}) async-start(), calls=%async_computation.1 | async-start | bytes 1638400 | tf_op jit(solution)/shard_map/reduce_scatter | solution.py:166
  7.2 3.2 %copy-start.5 = (bf16[128,5120]{1,0:T(8,128)(2,1)S(1)}, bf16[128,5120]{1,0:T(8,128)(2,1)}, u32[]{:S(2)}) copy-start(bf16[128,5120]{1,0:T(8,128)(2,1)} %param.10) | copy-start | bytes 3932164
  10.5 9.6 %copy-start.15 = (s32[8]{0:T(128)S(1)}, s32[8]{0:T(128)}, u32[]{:S(2)}) copy-start(s32[8]{0:T(128)} %param.16) | copy-start | bytes 100
  10.5 11.4 %copy-start.10 = (bf16[2,128,256]{2,1,0:T(8,128)(2,1)S(1)}, bf16[2,128,256]{2,1,0:T(8,128)(2,1)}, u32[]{:S(2)}) copy-start(bf16[2,128,256]{2,1,0:T(8,128)(2,1)} %param.14) | copy-start | bytes 393220
  11.7 15.7 %collective-permute-start.1 = (bf16[2,128,256]{2,1,0:T(8,128)(2,1)}, bf16[2,128,256]{2,1,0:T(8,128)(2,1)}, u32[]{:S(2)}, u32[]{:S(2)}) collective-permute-start(bf16[2,128,256]{2,1,0:T(8,128)(2,1)} %get-tuple-element.26), channel_id=1, source_target_pairs={{0,8},{4,12},{8,16},{12,20},{16,24},{20,28},{24,0},{28,4},{1,9},{5... | collective-permute-start | bytes 393224 | tf_op jit(solution)/shard_map/ppermute | solution.py:15
  14.7 12.7 %collective-permute-start = (bf16[2,128,256]{2,1,0:T(8,128)(2,1)}, bf16[2,128,256]{2,1,0:T(8,128)(2,1)}, u32[]{:S(2)}, u32[]{:S(2)}) collective-permute-start(bf16[2,128,256]{2,1,0:T(8,128)(2,1)} %get-tuple-element.26), channel_id=1, source_target_pairs={{0,4},{4,8},{8,12},{12,16},{16,20},{20,24},{24,28},{28,0},{1,5},{5... | collective-permute-start | bytes 393224 | tf_op jit(solution)/shard_map/ppermute | solution.py:15
  16.2 13.7 %collective-permute-start.2 = (bf16[2,128,256]{2,1,0:T(8,128)(2,1)}, bf16[2,128,256]{2,1,0:T(8,128)(2,1)}, u32[]{:S(2)}, u32[]{:S(2)}) collective-permute-start(bf16[2,128,256]{2,1,0:T(8,128)(2,1)} %get-tuple-element.26), channel_id=1, source_target_pairs={{0,12},{4,16},{8,20},{12,24},{16,28},{20,0},{24,4},{28,8},{1,13},{... | collective-permute-start | bytes 393224 | tf_op jit(solution)/shard_map/ppermute | solution.py:15
  23.3 2.6 %copy-start.2 = (bf16[128,2048]{0,1:T(8,128)(2,1)}, bf16[128,2048]{0,1:T(8,128)(2,1)S(1)}, u32[]{:S(2)}) copy-start(bf16[128,2048]{0,1:T(8,128)(2,1)S(1)} %copy.105) | copy-start | bytes 1572868
  27.4 8.8 %copy-start.11 = (bf16[128]{0:T(256)(128)(2,1)}, bf16[128]{0:T(256)(128)(2,1)S(1)}, u32[]{:S(2)}) copy-start(bf16[128]{0:T(256)(128)(2,1)S(1)} %fusion.57) | copy-start | bytes 772
  33.3 2.1 %copy-start.1 = (f32[1,128,2,8,128]{1,4,3,2,0:T(8,128)S(1)}, f32[1,128,2,8,128]{1,4,3,2,0:T(8,128)}, u32[]{:S(2)}) copy-start(f32[1,128,2,8,128]{1,4,3,2,0:T(8,128)} %get-tuple-element.30) | copy-start | bytes 3145732
  33.3 0.6 copy-start.8
  35.4 1.1 %copy-start.14 = (f32[128]{0:T(128)S(1)}, f32[128]{0:T(128)}, u32[]{:S(2)}) copy-start(f32[128]{0:T(128)} %compare_convert_fusion) | copy-start | bytes 1540
  36.5 2.0 %copy-start.12 = (bf16[128]{0:T(256)(128)(2,1)S(1)}, bf16[128]{0:T(256)(128)(2,1)}, u32[]{:S(2)}) copy-start(bf16[128]{0:T(256)(128)(2,1)} %copy-done.11) | copy-start | bytes 772
  36.5 2.3 %copy-start.3 = (bf16[128,2048]{0,1:T(8,128)(2,1)S(1)}, bf16[128,2048]{0,1:T(8,128)(2,1)}, u32[]{:S(2)}) copy-start(bf16[128,2048]{0,1:T(8,128)(2,1)} %copy-done.2) | copy-start | bytes 1572868
  38.8 0.8 copy-start.6
  41.7 8.3 %collective-permute-start.3 = (bf16[2,128,256]{2,1,0:T(8,128)(2,1)S(1)}, bf16[2,128,256]{2,1,0:T(8,128)(2,1)S(1)}, u32[]{:S(2)}, u32[]{:S(2)}) collective-permute-start(bf16[2,128,256]{2,1,0:T(8,128)(2,1)S(1)} %get-tuple-element.16), channel_id=1, source_target_pairs={{0,28},{4,0},{8,4},{12,8},{16,12},{20,16},{24,20},{28,24},{1,29},{... | collective-permute-start | bytes 393224 | tf_op jit(solution)/shard_map/ppermute | solution.py:15
  41.8 8.2 %collective-permute-start.5 = (bf16[2,128,256]{2,1,0:T(8,128)(2,1)S(1)}, bf16[2,128,256]{2,1,0:T(8,128)(2,1)S(1)}, u32[]{:S(2)}, u32[]{:S(2)}) collective-permute-start(bf16[2,128,256]{2,1,0:T(8,128)(2,1)S(1)} %get-tuple-element.17), channel_id=1, source_target_pairs={{0,20},{4,24},{8,28},{12,0},{16,4},{20,8},{24,12},{28,16},{1,21},{... | collective-permute-start | bytes 393224 | tf_op jit(solution)/shard_map/ppermute | solution.py:15
  42.3 8.3 %collective-permute-start.4 = (bf16[2,128,256]{2,1,0:T(8,128)(2,1)S(1)}, bf16[2,128,256]{2,1,0:T(8,128)(2,1)S(1)}, u32[]{:S(2)}, u32[]{:S(2)}) collective-permute-start(bf16[2,128,256]{2,1,0:T(8,128)(2,1)S(1)} %get-tuple-element.18), channel_id=1, source_target_pairs={{0,24},{4,28},{8,0},{12,4},{16,8},{20,12},{24,16},{28,20},{1,25},{... | collective-permute-start | bytes 393224 | tf_op jit(solution)/shard_map/ppermute | solution.py:15
  50.7 1.7 %copy-start.4 = (bf16[5120,256]{1,0:T(8,128)(2,1)S(1)}, bf16[5120,256]{1,0:T(8,128)(2,1)}, u32[]{:S(2)}) copy-start(bf16[5120,256]{1,0:T(8,128)(2,1)} %param.12) | copy-start | bytes 7864324
  52.5 2.1 %copy-start.13 = (bf16[128]{0:T(256)(128)(2,1)S(1)}, bf16[128]{0:T(256)(128)(2,1)}, u32[]{:S(2)}) copy-start(bf16[128]{0:T(256)(128)(2,1)} %copy-done.11) | copy-start | bytes 772
  56.1 6.0 %copy-start.9 = (bf16[1,1,128,256]{2,3,1,0:T(8,128)(2,1)S(1)}, bf16[1,1,128,256]{2,3,1,0:T(8,128)(2,1)}, u32[]{:S(2)}) copy-start(bf16[1,1,128,256]{2,3,1,0:T(8,128)(2,1)} %copy-done.8) | copy-start | bytes 196612
  59.9 0.8 copy-start.7
Sparse Core Ops, SparseCore 0:
  54.7 31.1 reduce-scatter.1
where the time goes:
time: 93.3 us; the launch traced here: 92.7 us
  waiting for transfers between devices  29 us (31%)
  matrix products  20.6 us (22%)
  between operations  16.4 us (18%)
  local copies, waits for them, and re-layouts  11.3 us (12%)
  starting transfers between devices  8.92 us (10%)
  other arithmetic  6.47 us (7%)
    reduce_scatter x1, waiting for transfers between devices, local(): lax.psum_scatter(partial_grad.astype(jnp.bfloat16), 'tensor', scatter_dim...  19.4 us
    ppermute x6, waiting for transfers between devices, passed_along(): return lax.ppermute(value, axis, pairs)  9.64 us
    ppermute x6, starting transfers between devices, passed_along(): return lax.ppermute(value, axis, pairs)  8.88 us
    unnamed x35, local copies, waits for them, and re-layouts  6.32 us
    dot_general x1, matrix products, local(): jnp.dot(prompt_hidden, w_value, preferred_element_type=jnp.float32)  2.79 us
    dot_general x1, matrix products, local(): lax.dot_general(value_grad, w_value, contract, preferred_element_type=jnp...  2.07 us
    dot_general x1, matrix products, local(): jnp.einsum('srkgu,sukd->srkgd', own_weights, own_values, preferred_elemen...  1.92 us
  transfers between devices with their start and end apart: 7, of which 4 were waited for; matrix products, arithmetic and copies ran while one was open for 19% of the time, Pallas kernels for 0%

commit v1 on v0

v1 whole, which is shorter than its diff:
```python
import functools

import jax
import jax.numpy as jnp
from jax import lax
from jax.experimental import pallas as pl
from jax.experimental.pallas import tpu as pltpu
from jax.sharding import PartitionSpec as P

HD = 128
MASKED_SCORE = -1e30
PAIR = 2
PROJ_CHUNKS = 4
COL_CHUNKS = 5
MESH = pl.DeviceIdType.MESH
NT = (((1,), (1,)), ((), ()))
TN = (((0,), (0,)), ((), ()))


def dot_nt(a, b):
    return lax.dot_general(a, b, NT, preferred_element_type=jnp.float32)


def dot_tn(a, b):
    return lax.dot_general(a, b, TN, preferred_element_type=jnp.float32)


def dot_nn(a, b):
    return jnp.dot(a, b, preferred_element_type=jnp.float32)


def kernel(
    n_dp, n_tensor, window,
    hid_hbm, wk_hbm, wv_hbm, q_hbm, okv_hbm, cot_hbm, plen, rlen, offs, adv,
    attn_hbm, gq_hbm, gkv_hbm, gph_hbm,
    hid, wk, wv, q, cot, okv, fk, fv, e_own, gp_own, gs, m_own, l_own, d_own,
    p_pre, ds_pre, p_own, ds_own, ratio, delta_s,
    tx, mine, rx, attn, gq, gkv, gph, sib_tx, sib_rx, x_tx, x_rx, near,
    in_sem, out_sem, fo_send, fo_recv, fi_send, fi_recv, sib_send, sib_recv, x_send, x_recv,
):
    me = lax.axis_index("dp")
    t_me = lax.axis_index("tensor")
    n_x = n_tensor // 2
    x_me, core = lax.div(t_me, 2), lax.rem(t_me, 2)
    sibling = x_me * 2 + 1 - core
    rows, width = q.shape
    prefix_rows, depth = hid.shape
    kv_width = wk.shape[1]
    kv_heads = kv_width // HD
    pairs = width // HD // PAIR
    group_pairs = pairs // kv_heads
    scale = HD ** (-0.5)
    far = range(window - 1, 0, -1)

    def ahead(d):
        return (lax.rem(me + d, n_dp), t_me)

    def behind(d):
        return (lax.rem(me + n_dp - d, n_dp), t_me)

    def across(dx):
        return (me, lax.rem(x_me + dx, n_x) * 2 + core)

    barrier = pltpu.get_barrier_semaphore()
    partners = [ahead(d) for d in far] + [behind(d) for d in far]
    partners += [(me, sibling)] + [across(dx) for dx in range(1, n_x)]
    for partner in partners:
        pl.semaphore_signal(barrier, inc=1, device_id=partner, device_id_type=MESH)

    step = depth // PROJ_CHUNKS
    loads = {}

    def load(name, src, dst):
        copy = pltpu.make_async_copy(src, dst, in_sem.at[len(loads)])
        copy.start()
        loads[name] = copy

    for c in range(PROJ_CHUNKS):
        part = pl.ds(c * step, step)
        load(("h", c), hid_hbm.at[:, part], hid.at[:, part])
        load(("k", c), wk_hbm.at[part, :], wk.at[part, :])
    for c in range(PROJ_CHUNKS):
        part = pl.ds(c * step, step)
        load(("v", c), wv_hbm.at[part, :], wv.at[part, :])
    load("okv", okv_hbm, okv)
    load("q", q_hbm, q)
    load("cot", cot_hbm, cot)

    def projected(name, weight):
        total = None
        for c in range(PROJ_CHUNKS):
            if name == "k":
                loads[("h", c)].wait()
            loads[(name, c)].wait()
            part = pl.ds(c * step, step)
            term = dot_nn(hid[:, part], weight[part, :])
            total = term if total is None else total + term
        return total.astype(jnp.bfloat16)

    def send(src, dst, send_sem, recv_sem, device):
        copy = pltpu.make_async_remote_copy(
            src_ref=src, dst_ref=dst, send_sem=send_sem, recv_sem=recv_sem,
            device_id=device, device_id_type=MESH,
        )
        copy.start()
        return copy

    out_key = []
    out_value = []
    fk[0] = projected("k", wk)
    pl.semaphore_wait(barrier, len(partners))
    for d in far:
        out_key.append(send(fk.at[0], fk.at[d], fo_send.at[0, d], fo_recv.at[0, d], ahead(d)))
    fv[0] = projected("v", wv)
    for d in far:
        out_value.append(send(fv.at[0], fv.at[d], fo_send.at[1, d], fo_recv.at[1, d], ahead(d)))

    off = offs[0]
    owner = lax.rem(me - off + n_dp, n_dp)
    chosen_len = plen[owner]
    row_at = lax.broadcasted_iota(jnp.int32, (PAIR * rows, rows), 0)
    row_at = jnp.where(row_at >= rows, row_at - rows, row_at)
    key_at = lax.broadcasted_iota(jnp.int32, (PAIR * rows, rows), 1)
    causal = row_at >= key_at
    valid = jnp.where(row_at[:, :1] < rlen[0], 1.0, 0.0)
    factor = valid * adv[0].astype(jnp.float32)
    prefix_ok = lax.broadcasted_iota(jnp.int32, (PAIR * rows, prefix_rows), 1) < chosen_len

    def head_cols(ref, p):
        return jnp.concatenate(
            [ref[:, (p * PAIR + u) * HD:(p * PAIR + u + 1) * HD] for u in range(PAIR)], axis=0
        )

    def put_cols(ref, p, value):
        for u in range(PAIR):
            ref[:, (p * PAIR + u) * HD:(p * PAIR + u + 1) * HD] = value[u * rows:(u + 1) * rows]

    def cols(g):
        return slice(g * HD, (g + 1) * HD)

    for name in ("okv", "q", "cot"):
        loads[name].wait()
    for p in range(pairs):
        g = p // group_pairs
        s = dot_nt(head_cols(q, p), okv[0, :, cols(g)]) * scale
        s = jnp.where(causal, s, MASKED_SCORE)
        m = jnp.max(s, axis=1, keepdims=True)
        e = jnp.exp(s - m)
        grad = (head_cols(cot, p).astype(jnp.float32) * factor).astype(jnp.bfloat16)
        gp = dot_nt(grad, okv[1, :, cols(g)])
        gs[p] = grad
        e_own[p] = e
        gp_own[p] = gp
        m_own[p] = m
        l_own[p] = jnp.sum(e, axis=1, keepdims=True)
        d_own[p] = jnp.sum(e * gp, axis=1, keepdims=True)

    for copy in out_key + out_value:
        copy.wait_recv()
    back = []
    for g in range(kv_heads):
        keys = fk[off, :, cols(g)]
        values = fv[off, :, cols(g)]
        mine_pairs = range(g * group_pairs, (g + 1) * group_pairs)
        for p in mine_pairs:
            s = dot_nt(head_cols(q, p), keys) * scale
            s = jnp.where(prefix_ok, s, MASKED_SCORE)
            m = jnp.maximum(jnp.max(s, axis=1, keepdims=True), m_own[p])
            e = jnp.exp(s - m)
            a = jnp.exp(m_own[p] - m)
            r = 1.0 / (a * l_own[p] + jnp.sum(e, axis=1, keepdims=True))
            probs = e * r
            gp = dot_nt(gs[p], values)
            a = a * r
            delta = jnp.sum(probs * gp, axis=1, keepdims=True) + a * d_own[p]
            p_pre[p] = probs.astype(jnp.bfloat16)
            ds_pre[p] = (probs * (gp - delta)).astype(jnp.bfloat16)
            ratio[p] = a
            delta_s[p] = delta
        q_all = jnp.concatenate([head_cols(q, p) for p in mine_pairs], axis=0)
        ds_all = jnp.concatenate([ds_pre[p] for p in mine_pairs], axis=0)
        p_all = jnp.concatenate([p_pre[p] for p in mine_pairs], axis=0)
        g_all = jnp.concatenate([gs[p] for p in mine_pairs], axis=0)
        both = [dot_tn(ds_all, q_all) * scale, dot_tn(p_all, g_all)]
        for i in range(2):
            for d in range(window):
                share = both[i] * jnp.where(off == d, 1.0, 0.0)
                if d == 0:
                    mine[g, i] = share
                else:
                    tx[d, g, i] = share.astype(jnp.bfloat16)
        for d in far:
            back.append(
                send(tx.at[d, g], rx.at[d, g], fi_send.at[g, d], fi_recv.at[g, d], behind(d))
            )

    stores = []

    def store(src, dst):
        copy = pltpu.make_async_copy(src, dst, out_sem.at[len(stores)])
        copy.start()
        stores.append(copy)

    for g in range(kv_heads):
        mine_pairs = range(g * group_pairs, (g + 1) * group_pairs)
        keys = jnp.concatenate([fk[off, :, cols(g)], okv[0, :, cols(g)]], axis=0)
        values = jnp.concatenate([fv[off, :, cols(g)], okv[1, :, cols(g)]], axis=0)
        for p in mine_pairs:
            probs = e_own[p] * ratio[p]
            ds = (probs * (gp_own[p] - delta_s[p])).astype(jnp.bfloat16)
            probs = probs.astype(jnp.bfloat16)
            p_own[p] = probs
            ds_own[p] = ds
            out = dot_nn(jnp.concatenate([p_pre[p], probs], axis=1), values) * valid
            put_cols(attn, p, out.astype(jnp.bfloat16))
            grad = dot_nn(jnp.concatenate([ds_pre[p], ds], axis=1), keys) * scale
            put_cols(gq, p, grad.astype(jnp.bfloat16))
        q_all = jnp.concatenate([head_cols(q, p) for p in mine_pairs], axis=0)
        ds_all = jnp.concatenate([ds_own[p] for p in mine_pairs], axis=0)
        p_all = jnp.concatenate([p_own[p] for p in mine_pairs], axis=0)
        g_all = jnp.concatenate([gs[p] for p in mine_pairs], axis=0)
        gkv[0, :, cols(g)] = (dot_tn(ds_all, q_all) * scale).astype(jnp.bfloat16)
        gkv[1, :, cols(g)] = dot_tn(p_all, g_all).astype(jnp.bfloat16)
    store(attn, attn_hbm)
    store(gq, gq_hbm)
    store(gkv, gkv_hbm)

    for copy in back:
        copy.wait_recv()
    summed = [[], []]
    for g in range(kv_heads):
        for i in range(2):
            total = mine[g, i]
            for d in range(1, window):
                total = total + rx[d, g, i].astype(jnp.float32)
            summed[i].append(total.astype(jnp.bfloat16))
    key_grad = jnp.concatenate(summed[0], axis=1)
    value_grad = jnp.concatenate(summed[1], axis=1)
    block = depth // n_tensor
    chunk = block // COL_CHUNKS

    def partial(dx, to_core, c):
        at = (lax.rem(x_me + dx, n_x) * 2 + to_core) * block + c * chunk
        part = pl.ds(pl.multiple_of(at, chunk), chunk)
        return dot_nt(key_grad, wk[part, :]) + dot_nt(value_grad, wv[part, :])

    to_sibling = {}
    to_across = []
    for dx in list(range(1, n_x)) + [0]:
        for c in range(COL_CHUNKS):
            sib_tx[dx, c] = partial(dx, 1 - core, c).astype(jnp.bfloat16)
            to_sibling[dx, c] = send(
                sib_tx.at[dx, c], sib_rx.at[dx, c], sib_send.at[dx, c], sib_recv.at[dx, c],
                (me, sibling),
            )
        for c in range(COL_CHUNKS):
            own = partial(dx, core, c)
            to_sibling[dx, c].wait_recv()
            own = own + sib_rx[dx, c].astype(jnp.float32)
            if dx == 0:
                near[c] = own
            else:
                x_tx[dx, c] = own.astype(jnp.bfloat16)
                to_across.append(
                    send(
                        x_tx.at[dx, c], x_rx.at[dx, c], x_send.at[dx, c], x_recv.at[dx, c],
                        across(dx),
                    )
                )
    for c in range(COL_CHUNKS):
        own = near[c]
        for dx in range(1, n_x):
            to_across[(dx - 1) * COL_CHUNKS + c].wait_recv()
            own = own + x_rx[dx, c].astype(jnp.float32)
        gph[:, c * chunk:(c + 1) * chunk] = own.astype(jnp.bfloat16)
    store(gph, gph_hbm)
    for copy in out_key + out_value + back + list(to_sibling.values()) + to_across:
        copy.wait_send()
    for copy in stores:
        copy.wait()


def local(
    prompt_hidden, w_key, w_value, resp_query, resp_kv, cotangent,
    prompt_len, resp_len, offsets, advantage,
):
    n_dp, n_tensor = lax.axis_size("dp"), lax.axis_size("tensor")
    window = min(8, n_dp // 2)
    n_x = n_tensor // 2
    rows, width = resp_query.shape
    prefix_rows, depth = prompt_hidden.shape
    kv_width = w_key.shape[1]
    kv_heads = kv_width // HD
    pairs = width // HD // PAIR
    stacked = PAIR * rows
    block = depth // n_tensor
    chunk = block // COL_CHUNKS
    bf, f32 = jnp.bfloat16, jnp.float32
    vmem = pltpu.VMEM
    scratch = [
        vmem((prefix_rows, depth), bf),
        vmem((depth, kv_width), bf),
        vmem((depth, kv_width), bf),
        vmem((rows, width), bf),
        vmem((rows, width), bf),
        vmem((2, rows, kv_width), bf),
        vmem((window, prefix_rows, kv_width), bf),
        vmem((window, prefix_rows, kv_width), bf),
        vmem((pairs, stacked, rows), f32),
        vmem((pairs, stacked, rows), f32),
        vmem((pairs, stacked, HD), bf),
        vmem((pairs, stacked, 1), f32),
        vmem((pairs, stacked, 1), f32),
        vmem((pairs, stacked, 1), f32),
        vmem((pairs, stacked, prefix_rows), bf),
        vmem((pairs, stacked, prefix_rows), bf),
        vmem((pairs, stacked, rows), bf),
        vmem((pairs, stacked, rows), bf),
        vmem((pairs, stacked, 1), f32),
        vmem((pairs, stacked, 1), f32),
        vmem((window, kv_heads, 2, prefix_rows, HD), bf),
        vmem((kv_heads, 2, prefix_rows, HD), f32),
        vmem((window, kv_heads, 2, prefix_rows, HD), bf),
        vmem((rows, width), bf),
        vmem((rows, width), bf),
        vmem((2, rows, kv_width), bf),
        vmem((prefix_rows, block), bf),
        vmem((n_x, COL_CHUNKS, prefix_rows, chunk), bf),
        vmem((n_x, COL_CHUNKS, prefix_rows, chunk), bf),
        vmem((n_x, COL_CHUNKS, prefix_rows, chunk), bf),
        vmem((n_x, COL_CHUNKS, prefix_rows, chunk), bf),
        vmem((COL_CHUNKS, prefix_rows, chunk), f32),
        pltpu.SemaphoreType.DMA((3 * PROJ_CHUNKS + 3,)),
        pltpu.SemaphoreType.DMA((4,)),
        pltpu.SemaphoreType.DMA((2, window)),
        pltpu.SemaphoreType.DMA((2, window)),
        pltpu.SemaphoreType.DMA((kv_heads, window)),
        pltpu.SemaphoreType.DMA((kv_heads, window)),
        pltpu.SemaphoreType.DMA((n_x, COL_CHUNKS)),
        pltpu.SemaphoreType.DMA((n_x, COL_CHUNKS)),
        pltpu.SemaphoreType.DMA((n_x, COL_CHUNKS)),
        pltpu.SemaphoreType.DMA((n_x, COL_CHUNKS)),
    ]
    anywhere = pl.BlockSpec(memory_space=pl.ANY)
    scalars = pl.BlockSpec(memory_space=pltpu.SMEM)
    return pl.pallas_call(
        functools.partial(kernel, n_dp, n_tensor, window),
        out_shape=(
            jax.ShapeDtypeStruct((rows, width), bf),
            jax.ShapeDtypeStruct((rows, width), bf),
            jax.ShapeDtypeStruct((2, rows, kv_width), bf),
            jax.ShapeDtypeStruct((prefix_rows, block), bf),
        ),
        in_specs=[anywhere] * 6 + [scalars] * 4,
        out_specs=(anywhere,) * 4,
        scratch_shapes=scratch,
        compiler_params=pltpu.CompilerParams(
            collective_id=0, has_side_effects=True, vmem_limit_bytes=56 * 2**20
        ),
    )(
        prompt_hidden, w_key, w_value, resp_query, resp_kv, cotangent,
        prompt_len, resp_len, offsets, advantage,
    )


def solution(mesh):
    placed = (
        P("dp", None),
        P(None, "tensor"),
        P(None, "tensor"),
        P("dp", "tensor"),
        P(None, "dp", "tensor"),
        P("dp", "tensor"),
        P(),
        P("dp"),
        P("dp"),
        P("dp"),
    )
    return jax.shard_map(
        local,
        mesh=mesh,
        in_specs=placed,
        out_specs=(
            P("dp", "tensor"),
            P("dp", "tensor"),
            P(None, "dp", "tensor"),
            P("dp", "tensor"),
        ),
        check_vma=False,
    )
```

time: 93.3 us -> 53 us (0.57)
  the two profiles are of different devices: /device:TPU:0 before, /device:TPU:28 now
where the time goes in v1:
time: 53 us; the launch traced here: 52 us
  Pallas kernels  42.4 us (80%)
  local copies, waits for them, and re-layouts  7.05 us (13%)
  between operations  2.58 us (5%)
    pallas_call x1, Pallas kernels, local(): pl.pallas_call(functools.partial(kernel, n_dp, n_tensor, window), out_sha...  42.4 us
    unnamed x4, local copies, waits for them, and re-layouts  7.05 us

profile of v1, /device:TPU:28, one launch (start us, length us, event | category | flops | bytes accessed | tf_op | source)
XLA Modules:
  0.0 52.0 jit_solution(11512470169887672978)
XLA Ops:
  2.6 42.4 %shard_map.129 = (bf16[128,2048]{1,0:T(8,128)(2,1)}, bf16[128,2048]{1,0:T(8,128)(2,1)}, bf16[2,128,256]{2,1,0:T(8,128)(2,1)}, bf16[128,1280]{1,0:T(8,128)(2,1)}) custom-call(bf16[128,5120]{1,0:T(8,128)(2,1)} %hid_hbm.1, bf16[5120,256]{1,0:T(8,128)(2,1)} %wk_hbm.1, bf16[5120,256]{1,0:T(8,128)(2,1)} %wv_hbm.1, bf16[128,2048]{1,0:T(8,128)(2,1)} %q_hbm.1, ...), custom_call_target="tpu_custom_call" | custom-call | tf_op jit(solution)/shard_map/pallas_call | solution.py:346
  45.0 1.9 %copy.21 = bf16[128,2048]{1,0:T(8,128)(2,1)} copy(bf16[128,2048]{1,0:T(8,128)(2,1)} %get-tuple-element.8) | data formatting | bytes 1048576
  46.9 1.9 %copy.22 = bf16[128,2048]{1,0:T(8,128)(2,1)} copy(bf16[128,2048]{1,0:T(8,128)(2,1)} %get-tuple-element.9) | data formatting | bytes 1048576
  48.7 1.6 %copy.23 = bf16[2,128,256]{2,1,0:T(8,128)(2,1)} copy(bf16[2,128,256]{2,1,0:T(8,128)(2,1)} %get-tuple-element.10) | data formatting | bytes 262144
  50.3 1.7 %copy.24 = bf16[128,1280]{1,0:T(8,128)(2,1)} copy(bf16[128,1280]{1,0:T(8,128)(2,1)} %get-tuple-element.11) | data formatting | bytes 655360

commit v2 on v1

--- a/solution.py
+++ b/solution.py
@@ -12,6 +12,7 @@
 PAIR = 2
 PROJ_CHUNKS = 4
 COL_CHUNKS = 5
+PARTS = 2
 MESH = pl.DeviceIdType.MESH
 NT = (((1,), (1,)), ((), ()))
 TN = (((0,), (0,)), ((), ()))
@@ -33,7 +34,7 @@
     n_dp, n_tensor, window,
     hid_hbm, wk_hbm, wv_hbm, q_hbm, okv_hbm, cot_hbm, plen, rlen, offs, adv,
     attn_hbm, gq_hbm, gkv_hbm, gph_hbm,
-    hid, wk, wv, q, cot, okv, fk, fv, e_own, gp_own, gs, m_own, l_own, d_own,
+    hid, wk, wv, q, cot, okv, kv, chosen, e_own, gp_own, gs, m_own, l_own, d_own,
     p_pre, ds_pre, p_own, ds_own, ratio, delta_s,
     tx, mine, rx, attn, gq, gkv, gph, sib_tx, sib_rx, x_tx, x_rx, near,
     in_sem, out_sem, fo_send, fo_recv, fi_send, fi_recv, sib_send, sib_recv, x_send, x_recv,
@@ -105,15 +106,17 @@
         copy.start()
         return copy
 
-    out_key = []
-    out_value = []
-    fk[0] = projected("k", wk)
+    for i, (name, weight) in enumerate((("k", wk), ("v", wv))):
+        block = projected(name, weight)
+        for g in range(kv_heads):
+            kv[0, g, i] = block[:, g * HD:(g + 1) * HD]
     pl.semaphore_wait(barrier, len(partners))
-    for d in far:
-        out_key.append(send(fk.at[0], fk.at[d], fo_send.at[0, d], fo_recv.at[0, d], ahead(d)))
-    fv[0] = projected("v", wv)
-    for d in far:
-        out_value.append(send(fv.at[0], fv.at[d], fo_send.at[1, d], fo_recv.at[1, d], ahead(d)))
+    out = {}
+    for g in range(kv_heads):
+        for d in far:
+            out[g, d] = send(
+                kv.at[0, g], kv.at[d, g], fo_send.at[g, d], fo_recv.at[g, d], ahead(d)
+            )
 
     off = offs[0]
     owner = lax.rem(me - off + n_dp, n_dp)
@@ -155,12 +158,28 @@
         l_own[p] = jnp.sum(e, axis=1, keepdims=True)
         d_own[p] = jnp.sum(e * gp, axis=1, keepdims=True)
 
-    for copy in out_key + out_value:
-        copy.wait_recv()
-    back = []
+    back = {}
+    part_rows = prefix_rows // PARTS
+
+    def send_back(g, part):
+        for d in far:
+            back[g, part, d] = send(
+                tx.at[d, part, g], rx.at[d, part, g],
+                fi_send.at[d, part, g], fi_recv.at[d, part, g], behind(d),
+            )
+
     for g in range(kv_heads):
-        keys = fk[off, :, cols(g)]
-        values = fv[off, :, cols(g)]
+        for d in far:
+            out[g, d].wait_recv()
+        keys, values = [
+            sum(
+                kv[d, g, i].astype(jnp.float32) * jnp.where(off == d, 1.0, 0.0)
+                for d in range(window)
+            ).astype(jnp.bfloat16)
+            for i in range(2)
+        ]
+        chosen[g, 0] = keys
+        chosen[g, 1] = values
         mine_pairs = range(g * group_pairs, (g + 1) * group_pairs)
         for p in mine_pairs:
             s = dot_nt(head_cols(q, p), keys) * scale
@@ -185,14 +204,16 @@
         for i in range(2):
             for d in range(window):
                 share = both[i] * jnp.where(off == d, 1.0, 0.0)
-                if d == 0:
-                    mine[g, i] = share
-                else:
-                    tx[d, g, i] = share.astype(jnp.bfloat16)
-        for d in far:
-            back.append(
-                send(tx.at[d, g], rx.at[d, g], fi_send.at[g, d], fi_recv.at[g, d], behind(d))
-            )
+                for part in range(PARTS):
+                    piece = share[part * part_rows:(part + 1) * part_rows]
+                    if d == 0:
+                        mine[part, g, i] = piece
+                    else:
+                        tx[d, part, g, i] = piece.astype(jnp.bfloat16)
+        send_back(g, 0)
+    for part in range(1, PARTS):
+        for g in range(kv_heads):
+            send_back(g, part)
 
     stores = []
 
@@ -201,10 +222,10 @@
         copy.start()
         stores.append(copy)
 
-    for g in range(kv_heads):
+    def rest(g):
         mine_pairs = range(g * group_pairs, (g + 1) * group_pairs)
-        keys = jnp.concatenate([fk[off, :, cols(g)], okv[0, :, cols(g)]], axis=0)
-        values = jnp.concatenate([fv[off, :, cols(g)], okv[1, :, cols(g)]], axis=0)
+        keys = jnp.concatenate([chosen[g, 0], okv[0, :, cols(g)]], axis=0)
+        values = jnp.concatenate([chosen[g, 1], okv[1, :, cols(g)]], axis=0)
         for p in mine_pairs:
             probs = e_own[p] * ratio[p]
             ds = (probs * (gp_own[p] - delta_s[p])).astype(jnp.bfloat16)
@@ -221,62 +242,90 @@
         g_all = jnp.concatenate([gs[p] for p in mine_pairs], axis=0)
         gkv[0, :, cols(g)] = (dot_tn(ds_all, q_all) * scale).astype(jnp.bfloat16)
         gkv[1, :, cols(g)] = dot_tn(p_all, g_all).astype(jnp.bfloat16)
+
+    for g in range(kv_heads):
+        rest(g)
     store(attn, attn_hbm)
     store(gq, gq_hbm)
     store(gkv, gkv_hbm)
 
-    for copy in back:
-        copy.wait_recv()
-    summed = [[], []]
-    for g in range(kv_heads):
-        for i in range(2):
-            total = mine[g, i]
-            for d in range(1, window):
-                total = total + rx[d, g, i].astype(jnp.float32)
-            summed[i].append(total.astype(jnp.bfloat16))
-    key_grad = jnp.concatenate(summed[0], axis=1)
-    value_grad = jnp.concatenate(summed[1], axis=1)
     block = depth // n_tensor
     chunk = block // COL_CHUNKS
-
-    def partial(dx, to_core, c):
-        at = (lax.rem(x_me + dx, n_x) * 2 + to_core) * block + c * chunk
-        part = pl.ds(pl.multiple_of(at, chunk), chunk)
-        return dot_nt(key_grad, wk[part, :]) + dot_nt(value_grad, wv[part, :])
-
     to_sibling = {}
-    to_across = []
-    for dx in list(range(1, n_x)) + [0]:
+    to_across = {}
+
+    def project_back(part):
+        grads = [[], []]
+        for g in range(kv_heads):
+            for d in far:
+                back[g, part, d].wait_recv()
+            for i in range(2):
+                total = mine[part, g, i]
+                for d in range(1, window):
+                    total = total + rx[d, part, g, i].astype(jnp.float32)
+                grads[i].append(total.astype(jnp.bfloat16))
+        key_grad = jnp.concatenate(grads[0], axis=1)
+        value_grad = jnp.concatenate(grads[1], axis=1)
+
+        def partial(dx, to_core, c):
+            at = (lax.rem(x_me + dx, n_x) * 2 + to_core) * block + c * chunk
+            at = pl.ds(pl.multiple_of(at, chunk), chunk)
+            return dot_nt(key_grad, wk[at, :]) + dot_nt(value_grad, wv[at, :])
+
+        for dx in list(range(1, n_x)) + [0]:
+            for c in range(COL_CHUNKS):
+                sib_tx[part, dx, c] = partial(dx, 1 - core, c).astype(jnp.bfloat16)
+                to_sibling[part, dx, c] = send(
+                    sib_tx.at[part, dx, c], sib_rx.at[part, dx, c],
+                    sib_send.at[part, dx, c], sib_recv.at[part, dx, c], (me, sibling),
+                )
+            for c in range(COL_CHUNKS):
+                own = partial(dx, core, c)
+                to_sibling[part, dx, c].wait_recv()
+                own = own + sib_rx[part, dx, c].astype(jnp.float32)
+                if dx == 0:
+                    near[part, c] = own
+                else:
+                    x_tx[part, dx, c] = own.astype(jnp.bfloat16)
+                    to_across[part, dx, c] = send(
+                        x_tx.at[part, dx, c], x_rx.at[part, dx, c],
+                        x_send.at[part, dx, c], x_recv.at[part, dx, c], across(dx),
+                    )
+
+    for part in range(PARTS):
+        project_back(part)
+    for part in range(PARTS):
+        at = slice(part * part_rows, (part + 1) * part_rows)
         for c in range(COL_CHUNKS):
-            sib_tx[dx, c] = partial(dx, 1 - core, c).astype(jnp.bfloat16)
-            to_sibling[dx, c] = send(
-                sib_tx.at[dx, c], sib_rx.at[dx, c], sib_send.at[dx, c], sib_recv.at[dx, c],
-                (me, sibling),
-            )
-        for c in range(COL_CHUNKS):
-            own = partial(dx, core, c)
-            to_sibling[dx, c].wait_recv()
-            own = own + sib_rx[dx, c].astype(jnp.float32)
-            if dx == 0:
-                near[c] = own
-            else:
-                x_tx[dx, c] = own.astype(jnp.bfloat16)
-                to_across.append(
-                    send(
-                        x_tx.at[dx, c], x_rx.at[dx, c], x_send.at[dx, c], x_recv.at[dx, c],
-                        across(dx),
-                    )
-                )
-    for c in range(COL_CHUNKS):
-        own = near[c]
-        for dx in range(1, n_x):
-            to_across[(dx - 1) * COL_CHUNKS + c].wait_recv()
-            own = own + x_rx[dx, c].astype(jnp.float32)
-        gph[:, c * chunk:(c + 1) * chunk] = own.astype(jnp.bfloat16)
+            own = near[part, c]
+            for dx in range(1, n_x):
+                to_across[part, dx, c].wait_recv()
+                own = own + x_rx[part, dx, c].astype(jnp.float32)
+            gph[at, c * chunk:(c + 1) * chunk] = own.astype(jnp.bfloat16)
     store(gph, gph_hbm)
-    for copy in out_key + out_value + back + list(to_sibling.values()) + to_across:
-        copy.wait_send()
+    for group in (out, back, to_sibling, to_across):
+        for copy in group.values():
+            copy.wait_send()
     for copy in stores:
+        copy.wait()
+
+
+def hand_over(*refs):
+    sources, targets, held, in_sem, out_sem = refs[:4], refs[4:8], refs[8:12], refs[12], refs[13]
+    ins = [
+        pltpu.make_async_copy(source, slot, in_sem.at[i])
+        for i, (source, slot) in enumerate(zip(sources, held))
+    ]
+    outs = [
+        pltpu.make_async_copy(slot, target, out_sem.at[i])
+        for i, (slot, target) in enumerate(zip(held, targets))
+    ]
+    for copy in ins:
+        copy.start()
+    for came, goes in zip(ins, outs):
+        came.wait()
+        goes.start()
+    for copy in outs:
         copy.wait()
 
 
@@ -295,6 +344,7 @@
     stacked = PAIR * rows
     block = depth // n_tensor
     chunk = block // COL_CHUNKS
+    part_rows = prefix_rows // PARTS
     bf, f32 = jnp.bfloat16, jnp.float32
     vmem = pltpu.VMEM
     scratch = [
@@ -304,8 +354,8 @@
         vmem((rows, width), bf),
         vmem((rows, width), bf),
         vmem((2, rows, kv_width), bf),
-        vmem((window, prefix_rows, kv_width), bf),
-        vmem((window, prefix_rows, kv_width), bf),
+        vmem((window, kv_heads, 2, prefix_rows, HD), bf),
+        vmem((kv_heads, 2, prefix_rows, HD), bf),
         vmem((pairs, stacked, rows), f32),
         vmem((pairs, stacked, rows), f32),
         vmem((pairs, stacked, HD), bf),
@@ -318,32 +368,32 @@
         vmem((pairs, stacked, rows), bf),
         vmem((pairs, stacked, 1), f32),
         vmem((pairs, stacked, 1), f32),
-        vmem((window, kv_heads, 2, prefix_rows, HD), bf),
-        vmem((kv_heads, 2, prefix_rows, HD), f32),
-        vmem((window, kv_heads, 2, prefix_rows, HD), bf),
+        vmem((window, PARTS, kv_heads, 2, part_rows, HD), bf),
+        vmem((PARTS, kv_heads, 2, part_rows, HD), f32),
+        vmem((window, PARTS, kv_heads, 2, part_rows, HD), bf),
         vmem((rows, width), bf),
         vmem((rows, width), bf),
         vmem((2, rows, kv_width), bf),
         vmem((prefix_rows, block), bf),
-        vmem((n_x, COL_CHUNKS, prefix_rows, chunk), bf),
-        vmem((n_x, COL_CHUNKS, prefix_rows, chunk), bf),
-        vmem((n_x, COL_CHUNKS, prefix_rows, chunk), bf),
-        vmem((n_x, COL_CHUNKS, prefix_rows, chunk), bf),
-        vmem((COL_CHUNKS, prefix_rows, chunk), f32),
+        vmem((PARTS, n_x, COL_CHUNKS, part_rows, chunk), bf),
+        vmem((PARTS, n_x, COL_CHUNKS, part_rows, chunk), bf),
+        vmem((PARTS, n_x, COL_CHUNKS, part_rows, chunk), bf),
+        vmem((PARTS, n_x, COL_CHUNKS, part_rows, chunk), bf),
+        vmem((PARTS, COL_CHUNKS, part_rows, chunk), f32),
         pltpu.SemaphoreType.DMA((3 * PROJ_CHUNKS + 3,)),
         pltpu.SemaphoreType.DMA((4,)),
-        pltpu.SemaphoreType.DMA((2, window)),
-        pltpu.SemaphoreType.DMA((2, window)),
         pltpu.SemaphoreType.DMA((kv_heads, window)),
         pltpu.SemaphoreType.DMA((kv_heads, window)),
-        pltpu.SemaphoreType.DMA((n_x, COL_CHUNKS)),
-        pltpu.SemaphoreType.DMA((n_x, COL_CHUNKS)),
-        pltpu.SemaphoreType.DMA((n_x, COL_CHUNKS)),
-        pltpu.SemaphoreType.DMA((n_x, COL_CHUNKS)),
+        pltpu.SemaphoreType.DMA((window, PARTS, kv_heads)),
+        pltpu.SemaphoreType.DMA((window, PARTS, kv_heads)),
+        pltpu.SemaphoreType.DMA((PARTS, n_x, COL_CHUNKS)),
+        pltpu.SemaphoreType.DMA((PARTS, n_x, COL_CHUNKS)),
+        pltpu.SemaphoreType.DMA((PARTS, n_x, COL_CHUNKS)),
+        pltpu.SemaphoreType.DMA((PARTS, n_x, COL_CHUNKS)),
     ]
     anywhere = pl.BlockSpec(memory_space=pl.ANY)
     scalars = pl.BlockSpec(memory_space=pltpu.SMEM)
-    return pl.pallas_call(
+    results = pl.pallas_call(
         functools.partial(kernel, n_dp, n_tensor, window),
         out_shape=(
             jax.ShapeDtypeStruct((rows, width), bf),
@@ -361,6 +411,14 @@
         prompt_hidden, w_key, w_value, resp_query, resp_kv, cotangent,
         prompt_len, resp_len, offsets, advantage,
     )
+    return pl.pallas_call(
+        hand_over,
+        out_shape=tuple(jax.ShapeDtypeStruct(a.shape, a.dtype) for a in results),
+        in_specs=[anywhere] * 4,
+        out_specs=(anywhere,) * 4,
+        scratch_shapes=[vmem(a.shape, a.dtype) for a in results]
+        + [pltpu.SemaphoreType.DMA((4,)), pltpu.SemaphoreType.DMA((4,))],
+    )(*results)
 
 
 def solution(mesh):

time: 53 us -> 46.8 us (0.88); the launches traced: 52 us -> 46.7 us
  local copies, waits for them, and re-layouts: 7.05 us -> 0 us
  Pallas kernels: 42.4 us -> 44.1 us
    unnamed x4 -> x0, local copies, waits for them, and re-layouts: 7.05 us -> none
    pallas_call x0 -> x1, Pallas kernels: none -> 2.22 us  [local(): pl.pallas_call(hand_over, out_shape=tuple((jax.ShapeDtypeStruct(a.shape,...]
    pallas_call x1, Pallas kernels: 42.4 us -> 41.9 us  [local(): pl.pallas_call(functools.partial(kernel, n_dp, n_tensor, window), out_sha...]
where the time goes in v2:
time: 46.8 us; the launch traced here: 46.7 us
  Pallas kernels  44.1 us (94%)
  between operations  2.58 us (6%)
    pallas_call x1, Pallas kernels, local(): pl.pallas_call(functools.partial(kernel, n_dp, n_tensor, window), out_sha...  41.9 us
    pallas_call x1, Pallas kernels, local(): pl.pallas_call(hand_over, out_shape=tuple((jax.ShapeDtypeStruct(a.shape,...  2.22 us

profile of v2, /device:TPU:28, one launch (start us, length us, event | category | flops | bytes accessed | tf_op | source)
XLA Modules:
  0.0 46.7 jit_solution(17081062726396915266)
XLA Ops:
  2.6 41.9 %shard_map.129 = (bf16[128,2048]{1,0:T(8,128)(2,1)}, bf16[128,2048]{1,0:T(8,128)(2,1)}, bf16[2,128,256]{2,1,0:T(8,128)(2,1)}, bf16[128,1280]{1,0:T(8,128)(2,1)}) custom-call(bf16[128,5120]{1,0:T(8,128)(2,1)} %hid_hbm.1, bf16[5120,256]{1,0:T(8,128)(2,1)} %wk_hbm.1, bf16[5120,256]{1,0:T(8,128)(2,1)} %wv_hbm.1, bf16[128,2048]{1,0:T(8,128)(2,1)} %q_hbm.1, ...), custom_call_target="tpu_custom_call" | custom-call | tf_op jit(solution)/shard_map/pallas_call | solution.py:396
  44.4 2.2 %shard_map.130 = (bf16[128,2048]{1,0:T(8,128)(2,1)}, bf16[128,2048]{1,0:T(8,128)(2,1)}, bf16[2,128,256]{2,1,0:T(8,128)(2,1)}, bf16[128,1280]{1,0:T(8,128)(2,1)}) custom-call(bf16[128,2048]{1,0:T(8,128)(2,1)} %get-tuple-element.8.refs_0_, bf16[128,2048]{1,0:T(8,128)(2,1)} %get-tuple-element.9.refs_1_, bf16[2,128,256]{2,1,0:T(8,128)(2,1)} %get-tuple-element.10.refs_2_, ...), custom_call_target="tpu_custom_call" | custom-call | tf_op jit(solution)/shard_map/pallas_call | solution.py:414

commit v3 on v2

--- a/solution.py
+++ b/solution.py
@@ -32,9 +32,9 @@
 
 def kernel(
     n_dp, n_tensor, window,
-    hid_hbm, wk_hbm, wv_hbm, q_hbm, okv_hbm, cot_hbm, plen, rlen, offs, adv,
+    hid_hbm, wk_hbm, wv_hbm, q_hbm, okv_hbm, cot_hbm, plen_hbm, rlen_hbm, offs_hbm, adv_hbm,
     attn_hbm, gq_hbm, gkv_hbm, gph_hbm,
-    hid, wk, wv, q, cot, okv, kv, chosen, e_own, gp_own, gs, m_own, l_own, d_own,
+    plen, rlen, offs, adv, hid, wk, wv, q, cot, okv, kv, chosen, e_own, gp_own, gs, m_own, l_own, d_own,
     p_pre, ds_pre, p_own, ds_own, ratio, delta_s,
     tx, mine, rx, attn, gq, gkv, gph, sib_tx, sib_rx, x_tx, x_rx, near,
     in_sem, out_sem, fo_send, fo_recv, fi_send, fi_recv, sib_send, sib_recv, x_send, x_recv,
@@ -86,6 +86,10 @@
     load("okv", okv_hbm, okv)
     load("q", q_hbm, q)
     load("cot", cot_hbm, cot)
+    small = {"plen": (plen_hbm, plen), "rlen": (rlen_hbm, rlen), "offs": (offs_hbm, offs)}
+    small["adv"] = (adv_hbm, adv)
+    for name in small:
+        load(name, *small[name])
 
     def projected(name, weight):
         total = None
@@ -118,6 +122,8 @@
                 kv.at[0, g], kv.at[d, g], fo_send.at[g, d], fo_recv.at[g, d], ahead(d)
             )
 
+    for name in small:
+        loads[name].wait()
     off = offs[0]
     owner = lax.rem(me - off + n_dp, n_dp)
     chosen_len = plen[owner]
@@ -347,7 +353,8 @@
     part_rows = prefix_rows // PARTS
     bf, f32 = jnp.bfloat16, jnp.float32
     vmem = pltpu.VMEM
-    scratch = [
+    scratch = [pltpu.SMEM(a.shape, a.dtype) for a in (prompt_len, resp_len, offsets, advantage)]
+    scratch += [
         vmem((prefix_rows, depth), bf),
         vmem((depth, kv_width), bf),
         vmem((depth, kv_width), bf),
@@ -380,7 +387,7 @@
         vmem((PARTS, n_x, COL_CHUNKS, part_rows, chunk), bf),
         vmem((PARTS, n_x, COL_CHUNKS, part_rows, chunk), bf),
         vmem((PARTS, COL_CHUNKS, part_rows, chunk), f32),
-        pltpu.SemaphoreType.DMA((3 * PROJ_CHUNKS + 3,)),
+        pltpu.SemaphoreType.DMA((3 * PROJ_CHUNKS + 7,)),
         pltpu.SemaphoreType.DMA((4,)),
         pltpu.SemaphoreType.DMA((kv_heads, window)),
         pltpu.SemaphoreType.DMA((kv_heads, window)),
@@ -392,7 +399,6 @@
         pltpu.SemaphoreType.DMA((PARTS, n_x, COL_CHUNKS)),
     ]
     anywhere = pl.BlockSpec(memory_space=pl.ANY)
-    scalars = pl.BlockSpec(memory_space=pltpu.SMEM)
     results = pl.pallas_call(
         functools.partial(kernel, n_dp, n_tensor, window),
         out_shape=(
@@ -401,7 +407,7 @@
             jax.ShapeDtypeStruct((2, rows, kv_width), bf),
             jax.ShapeDtypeStruct((prefix_rows, block), bf),
         ),
-        in_specs=[anywhere] * 6 + [scalars] * 4,
+        in_specs=[anywhere] * 10,
         out_specs=(anywhere,) * 4,
         scratch_shapes=scratch,
         compiler_params=pltpu.CompilerParams(

time: 46.8 us -> 46.2 us (0.987)
  Pallas kernels: 44.1 us -> 43.4 us
    pallas_call x1, Pallas kernels: 41.9 us -> 41.2 us  [local(): pl.pallas_call(functools.partial(kernel, n_dp, n_tensor, window), out_sha...]
where the time goes in v3:
time: 46.2 us; the launch traced here: 46 us
  Pallas kernels  43.4 us (94%)
  between operations  2.58 us (6%)
    pallas_call x1, Pallas kernels, local(): pl.pallas_call(functools.partial(kernel, n_dp, n_tensor, window), out_sha...  41.2 us
    pallas_call x1, Pallas kernels, local(): pl.pallas_call(hand_over, out_shape=tuple((jax.ShapeDtypeStruct(a.shape,...  2.22 us

profile of v3, /device:TPU:28, one launch (start us, length us, event | category | flops | bytes accessed | tf_op | source)
XLA Modules:
  0.0 46.0 jit_solution(10253505363342826621)
XLA Ops:
  2.6 41.2 %shard_map.129 = (bf16[128,2048]{1,0:T(8,128)(2,1)}, bf16[128,2048]{1,0:T(8,128)(2,1)}, bf16[2,128,256]{2,1,0:T(8,128)(2,1)}, bf16[128,1280]{1,0:T(8,128)(2,1)}) custom-call(bf16[128,5120]{1,0:T(8,128)(2,1)} %hid_hbm.1, bf16[5120,256]{1,0:T(8,128)(2,1)} %wk_hbm.1, bf16[5120,256]{1,0:T(8,128)(2,1)} %wv_hbm.1, bf16[128,2048]{1,0:T(8,128)(2,1)} %q_hbm.1, ...), custom_call_target="tpu_custom_call" | custom-call | tf_op jit(solution)/shard_map/pallas_call | solution.py:402
  43.8 2.2 %shard_map.130 = (bf16[128,2048]{1,0:T(8,128)(2,1)}, bf16[128,2048]{1,0:T(8,128)(2,1)}, bf16[2,128,256]{2,1,0:T(8,128)(2,1)}, bf16[128,1280]{1,0:T(8,128)(2,1)}) custom-call(bf16[128,2048]{1,0:T(8,128)(2,1)} %get-tuple-element.8.refs_0_, bf16[128,2048]{1,0:T(8,128)(2,1)} %get-tuple-element.9.refs_1_, bf16[2,128,256]{2,1,0:T(8,128)(2,1)} %get-tuple-element.10.refs_2_, ...), custom_call_target="tpu_custom_call" | custom-call | tf_op jit(solution)/shard_map/pallas_call | solution.py:420
